TPU v7x, 32 devices: a whole 2x2x4 slice. The times are simulated.
32 devices in a mesh: resp: 4 (over y, core), ctx: 8 (over z, x).
Axes of the slice: x: 2, y: 2, z: 4, core: 2. Of those that a mesh axis runs over, the one named last changes fastest.
Arguments:
- queries: bfloat16 [8, 2048, 8, 128], P('resp', 'ctx'), may hold values from -170 to 170
- prompt_keys: bfloat16 [128, 128], P('ctx'), may hold values from -6 to 6
- prompt_values: bfloat16 [128, 128], P('ctx'), may hold values from -6 to 6
- resp_keys: bfloat16 [8, 2048, 128], P('resp', 'ctx'), may hold values from -6 to 6
- resp_values: bfloat16 [8, 2048, 128], P('resp', 'ctx'), may hold values from -6 to 6
- upstream: bfloat16 [8, 2048, 8, 128], P('resp', 'ctx'), may hold values from -6 to 6
- behav_logp: float32 [8, 2048], P('resp', 'ctx'), may hold values from -2.5 to -0.1
- cur_logp: float32 [8, 2048], P('resp', 'ctx'), may hold values from -2.5 to -0.1
- advantages: float32 [8], P('resp'), may hold values from -4 to 4
- lengths: int32 [8], P('resp'), may hold values from 128 to 2048, as said below
Outputs:
- grad_queries: bfloat16 [8, 2048, 8, 128], P('resp', 'ctx')
- grad_resp_keys: bfloat16 [8, 2048, 128], P('resp', 'ctx')
- grad_resp_values: bfloat16 [8, 2048, 128], P('resp', 'ctx')
- grad_prompt_keys: float32 [128, 128], P('ctx')
- grad_prompt_values: float32 [128, 128], P('ctx')
Inputs may be any that keep to these rules, and one draw needn't show every extreme that they name: `lengths`: each length is a multiple of 128; in every draw one response has length 2048 and another has length 128.
All inputs are finite; a program needn't handle non-finite values.
Results may differ from a plain program's by a relative error of at most 0.024.
Values may be sent and summed in bfloat16 or wider, within the bound.
No kernel may reach another device: no remote copies, remote signals or barrier semaphores. Data moves between devices by JAX's collectives and lax.ppermute only.
A program may use at most 64 MiB of HBM per device.

v0:
```python
import jax
import jax.numpy as jnp
from jax import lax
from jax.sharding import PartitionSpec as P

RATIO_CAP = 2.0


def token_weights(advantages, behav_logp, cur_logp, lengths, positions, full_len):
    ratio = jnp.minimum(jnp.exp(cur_logp - behav_logp), RATIO_CAP)
    valid = (positions[None, :] < lengths[:, None]).astype(jnp.float32)
    spread = full_len / lengths.astype(jnp.float32)
    return -advantages[:, None] * ratio * valid * spread[:, None]


def attend_block(query_rows, grad_rows, keys_all, values_all, row_pos, col_pos, softmax_scale):
    scores = jnp.dot(query_rows, keys_all.T, preferred_element_type=jnp.float32) * softmax_scale
    scores = jnp.where(col_pos[None, :] <= row_pos[:, None], scores, -jnp.inf)
    row_max = jnp.max(scores, axis=1, keepdims=True)
    shifted = jnp.exp(scores - row_max)
    probs = lax.optimization_barrier(
        (shifted / jnp.sum(shifted, axis=1, keepdims=True)).astype(jnp.bfloat16)
    )
    attended = lax.optimization_barrier(
        jnp.dot(probs, values_all, preferred_element_type=jnp.float32).astype(jnp.bfloat16)
    )
    deltas = jnp.sum(grad_rows.astype(jnp.float32) * attended.astype(jnp.float32), axis=1)
    grad_probs = jnp.dot(grad_rows, values_all.T, preferred_element_type=jnp.float32)
    grad_scores = (probs.astype(jnp.float32) * (grad_probs - deltas[:, None])).astype(jnp.bfloat16)
    query_grad = (
        jnp.dot(grad_scores, keys_all, preferred_element_type=jnp.float32) * softmax_scale
    ).astype(jnp.bfloat16)
    return (probs, grad_scores, query_grad)


def per_device(
    queries,
    prompt_keys,
    prompt_values,
    resp_keys,
    resp_values,
    upstream,
    behav_logp,
    cur_logp,
    advantages,
    lengths,
):
    resp_dev, tok_dev, heads, head_dim = queries.shape
    softmax_scale = head_dim ** (-0.5)
    ctx_size = lax.axis_size("ctx")
    full_len = tok_dev * ctx_size
    local_prompt = prompt_keys.shape[0]
    all_prompt_keys, all_prompt_values, all_resp_keys, all_resp_values = (
        lax.all_gather(prompt_keys, "ctx", axis=0, tiled=True),
        lax.all_gather(prompt_values, "ctx", axis=0, tiled=True),
        lax.all_gather(resp_keys, "ctx", axis=1, tiled=True),
        lax.all_gather(resp_values, "ctx", axis=1, tiled=True),
    )
    prompt_len = all_prompt_keys.shape[0]
    positions = lax.axis_index("ctx") * tok_dev + jnp.arange(tok_dev, dtype=jnp.int32)
    weights = token_weights(advantages, behav_logp, cur_logp, lengths, positions, full_len)
    grad_out = (weights[:, :, None, None] * upstream.astype(jnp.float32)).astype(jnp.bfloat16)
    row_pos = jnp.repeat(positions, heads)
    col_pos = jnp.concatenate(
        [jnp.full((prompt_len,), -1, jnp.int32), jnp.arange(full_len, dtype=jnp.int32)]
    )
    query_rows = queries.reshape(resp_dev, tok_dev * heads, head_dim)
    grad_rows = grad_out.reshape(resp_dev, tok_dev * heads, head_dim)
    prob_list = []
    score_list = []
    query_list = []
    for member in range(resp_dev):
        keys_all = jnp.concatenate([all_prompt_keys, all_resp_keys[member]], 0)
        values_all = jnp.concatenate([all_prompt_values, all_resp_values[member]], 0)
        probs, grad_scores, query_grad = attend_block(
            query_rows[member],
            grad_rows[member],
            keys_all,
            values_all,
            row_pos,
            col_pos,
            softmax_scale,
        )
        prob_list.append(probs)
        score_list.append(grad_scores)
        query_list.append(query_grad)
    grad_queries = jnp.stack(query_list).reshape(queries.shape)

    def member_term(member, row_count, offset):
        score_cols = lax.dynamic_slice_in_dim(score_list[member], offset, row_count, 1)
        prob_cols = lax.dynamic_slice_in_dim(prob_list[member], offset, row_count, 1)
        key_part = (
            jnp.dot(score_cols.T, query_rows[member], preferred_element_type=jnp.float32)
            * softmax_scale
        )
        value_part = jnp.dot(prob_cols.T, grad_rows[member], preferred_element_type=jnp.float32)
        return jnp.concatenate([key_part, value_part], 1)

    row_count = tok_dev * lax.axis_size("ctx")
    part_list = []
    for member in range(resp_dev):
        part_list.append(member_term(member, row_count, prompt_len))
    response_sums = lax.psum_scatter(
        jnp.stack(part_list, 1).astype(jnp.bfloat16), "ctx", scatter_dimension=0, tiled=True
    ).astype(jnp.float32)
    response_grads = jnp.transpose(response_sums, (1, 0, 2)).astype(jnp.bfloat16)
    summed = member_term(0, local_prompt * lax.axis_size("ctx"), 0)
    member = 1
    summed = summed + member_term(member, local_prompt * lax.axis_size("ctx"), 0)
    ctx_share = lax.psum_scatter(
        summed.astype(jnp.bfloat16), "ctx", scatter_dimension=0, tiled=True
    ).astype(jnp.float32)
    prompt_total = lax.psum(ctx_share, "resp")
    return (
        grad_queries,
        response_grads[:, :, :head_dim],
        response_grads[:, :, head_dim:],
        prompt_total[:, :head_dim],
        prompt_total[:, head_dim:],
    )


def solution(mesh):
    placed = (
        P("resp", "ctx", None, None),
        P("ctx", None),
        P("ctx", None),
        P("resp", "ctx", None),
        P("resp", "ctx", None),
        P("resp", "ctx", None, None),
        P("resp", "ctx"),
        P("resp", "ctx"),
        P("resp"),
        P("resp"),
    )
    return jax.shard_map(
        per_device,
        mesh=mesh,
        in_specs=placed,
        out_specs=(
            P("resp", "ctx", None, None),
            P("resp", "ctx", None),
            P("resp", "ctx", None),
            P("ctx", None),
            P("ctx", None),
        ),
        check_vma=False,
    )
```

profile of v0, /device:TPU:0, one launch (start us, length us, event | category | flops | bytes accessed | tf_op | source)
XLA Modules:
  0.0 336.1 jit_solution(17351578604741329472)
XLA Ops:
  7.2 0.7 all-gather.3.cloned.1.call-update
  7.9 0.0 all-gather.5.cloned.1.call-start
  7.9 0.7 all-gather.5.cloned.1.call-update
  8.6 0.0 reduce-scatter.7.cloned.1.call-start
  8.7 32.4 %all_gather.12 = bf16[128,128]{1,0:T(8,128)(2,1)S(1)} all-gather(bf16[16,128]{1,0:T(8,128)(2,1)} %param.11), channel_id=1, replica_groups=mesh['resp'=4,'ctx'=8] {'ctx'}, dimensions={0}, use_global_device_ids=true | all-gather | bytes 36864 | tf_op jit(solution)/shard_map/all_gather | solution.py:54
  41.1 0.1 broadcast_in_dim.6
  41.2 0.1 le.9
  41.3 30.5 %all_gather.14 = bf16[128,128]{1,0:T(8,128)(2,1)S(1)} all-gather(bf16[16,128]{1,0:T(8,128)(2,1)} %param.12), channel_id=1, replica_groups=mesh['resp'=4,'ctx'=8] {'ctx'}, dimensions={0}, use_global_device_ids=true | all-gather | bytes 36864 | tf_op jit(solution)/shard_map/all_gather | solution.py:55
  71.9 0.7 convert_divide_fusion
  72.6 0.7 neg.4
  73.2 0.8 fusion.51
  74.0 1.8 multiply_convert_fusion.2
  75.8 1.6 slice_bitcast_fusion.5
  77.4 9.2 %fusion.63 = (f32[2048]{0:T(1024)S(1)}, f32[2048,2176]{0,1:T(8,128)}) fusion(bf16[2,256,8,128]{3,2,1,0:T(8,128)(2,1)} %param.10, bf16[128,128]{1,0:T(8,128)(2,1)S(1)} %all_gather.12, bf16[2048,128]{1,0:T(8,128)(2,1)S(1)} %get-tuple-element.24, s32[2048]{0:T(1024)S(1)} %le.9, s32[2176]{0:T(1024)} %constant.8.clone.1), kind=kOutput, calls=%fused_computation.86 | convolution fusion | flops 1159788544 | bytes 18935808 | tf_op jit(solution)/shard_map/dot_general | solution.py:17
  86.6 8.5 %fusion = f32[2048]{0:T(1024)S(1)} fusion(f32[2048,2176]{0,1:T(8,128)} %get-tuple-element.33, f32[2048]{0:T(1024)S(1)} %get-tuple-element.32), kind=kLoop, calls=%fused_computation.8 | loop fusion | flops 8910848 | bytes 17842176 | tf_op jit(solution)/shard_map/reduce_sum | solution.py:22
  95.1 10.3 %divide_convert_fusion.1 = bf16[2048,2176]{0,1:T(8,128)(2,1)} fusion(f32[2048,2176]{0,1:T(8,128)} %get-tuple-element.33, f32[2048]{0:T(1024)S(1)} %fusion, f32[2048]{0:T(1024)S(1)} %get-tuple-element.32), kind=kLoop, calls=%fused_computation.6 | loop fusion | flops 13369344 | bytes 26755072 | tf_op jit(solution)/shard_map/convert_element_type | solution.py:22
  105.5 2.2 slice_bitcast_fusion
  107.6 0.8 copy-done.4
  108.5 6.9 %convolution_convert_fusion.1 = bf16[2048,128]{1,0:T(8,128)(2,1)} fusion(bf16[2048,2176]{0,1:T(8,128)(2,1)} %divide_convert_fusion.1, bf16[128,128]{1,0:T(8,128)(2,1)S(1)} %all_gather.14, bf16[2048,128]{1,0:T(8,128)(2,1)S(1)} %get-tuple-element.23), kind=kOutput, calls=%fused_computation.29 | convolution fusion | flops 1142226944 | bytes 9994240 | tf_op jit(solution)/shard_map/dot_general | solution.py:25
  115.4 18.3 %fusion.62 = (f32[2048]{0:T(1024)S(1)}, f32[2048,2176]{0,1:T(8,128)}) fusion(bf16[2,256,8,128]{3,2,1,0:T(8,128)(2,1)S(1)} %copy-done.20, bf16[128,128]{1,0:T(8,128)(2,1)S(1)} %all_gather.12, bf16[2048,128]{1,0:T(8,128)(2,1)S(1)} %get-tuple-element.25, s32[2048]{0:T(1024)S(1)} %le.9, s32[2176]{0:T(1024)S(1)} %copy-done.21), kind=kOutput, calls=%fused_computation.85 | convolution fusion | flops 1159788544 | bytes 18935808 | tf_op jit(solution)/shard_map/dot_general | solution.py:17
  133.7 8.5 %fusion.1 = f32[2048]{0:T(1024)S(1)} fusion(f32[2048,2176]{0,1:T(8,128)} %get-tuple-element.31, f32[2048]{0:T(1024)S(1)} %get-tuple-element.30), kind=kLoop, calls=%fused_computation.9 | loop fusion | flops 8910848 | bytes 17842176 | tf_op jit(solution)/shard_map/reduce_sum | solution.py:22
  142.2 7.6 %divide_convert_fusion = bf16[2048,2176]{0,1:T(8,128)(2,1)S(1)} fusion(f32[2048,2176]{0,1:T(8,128)} %get-tuple-element.31, f32[2048]{0:T(1024)S(1)} %fusion.1, f32[2048]{0:T(1024)S(1)} %get-tuple-element.30), kind=kLoop, calls=%fused_computation.3 | loop fusion | flops 13369344 | bytes 26755072 | tf_op jit(solution)/shard_map/convert_element_type | solution.py:22
  149.8 2.2 fusion.35
  152.0 1.0 fusion.32
  153.0 2.7 convolution_convert_fusion
  155.7 1.0 multiply_reduce_fusion.1
  156.6 7.2 %multiply_convert_fusion.1 = bf16[2048,2176]{0,1:T(8,128)(2,1)} fusion(bf16[2048,2176]{0,1:T(8,128)(2,1)S(1)} %bitcast.59, f32[2048]{0:T(1024)} %get-tuple-element.20, bf16[128,128]{1,0:T(8,128)(2,1)} %copy-done.13, bf16[2048,128]{1,0:T(8,128)(2,1)} %copy-done.4, bf16[2,256,8,128]{3,2,1,0:T(8,128)(2,1)} %copy-done), kind=kOutput, calls=%fused_computation.5 | convolution fusion | flops 1159790592 | bytes 18915328 | tf_op jit(solution)/shard_map/dot_general | solution.py:28
  163.9 2.2 convolution_multiply_fusion.3
  166.0 6.6 %fusion.25 = bf16[2048,128]{1,0:T(8,128)(2,1)} fusion(bf16[2048,2176]{0,1:T(8,128)(2,1)} %multiply_convert_fusion.1, bf16[2,256,8,128]{3,2,1,0:T(8,128)(2,1)} %param.10), kind=kOutput, calls=%fused_computation.25 | convolution fusion | flops 1074266112 | bytes 9437184 | tf_op jit(solution)/shard_map/dot_general | solution.py:93
  172.6 7.2 %multiply_convert_fusion = bf16[2048,2176]{0,1:T(8,128)(2,1)} fusion(bf16[2048,2176]{0,1:T(8,128)(2,1)S(1)} %divide_convert_fusion, f32[2048]{0:T(1024)S(1)} %get-tuple-element.21, bf16[128,128]{1,0:T(8,128)(2,1)} %copy-done.13, bf16[2048,128]{1,0:T(8,128)(2,1)} %get-tuple-element.22, bf16[2,256,8,128]{3,2,1,0:T(8,128)(2,1)} %copy-done), kind=kOutput, calls=%fused_computation.2 | convolution fusion | flops 1159790592 | bytes 18915328 | tf_op jit(solution)/shard_map/dot_general | solution.py:28
  179.8 1.6 convolution_multiply_fusion.2
  181.5 6.8 %fusion.22 = bf16[2048,128]{1,0:T(8,128)(2,1)} fusion(bf16[2048,2176]{0,1:T(8,128)(2,1)} %multiply_convert_fusion, bf16[2,256,8,128]{3,2,1,0:T(8,128)(2,1)} %param.10), kind=kOutput, calls=%fused_computation.24 | convolution fusion | flops 1074266112 | bytes 9437184 | tf_op jit(solution)/shard_map/dot_general | solution.py:93
  188.3 3.2 fusion.16
  191.6 2.4 fusion.19
  194.0 0.7 copy.45
  194.8 0.3 reduce-scatter.5.cloned.1.call-start
  195.1 0.2 maximum_bitcast_fusion
  195.4 1.5 pad_maximum_fusion
  196.9 6.1 %fusion.31 = bf16[1,256,8,128]{3,2,1,0:T(8,128)(2,1)S(1)} fusion(bf16[2048,2176]{0,1:T(8,128)(2,1)} %multiply_convert_fusion.1, bf16[128,128]{1,0:T(8,128)(2,1)S(1)} %copy-done.19, bf16[2048,128]{1,0:T(8,128)(2,1)S(1)} %copy-done.8), kind=kOutput, calls=%fused_computation.33 | convolution fusion | flops 1142489088 | bytes 9994240 | tf_op jit(solution)/shard_map/dot_general | solution.py:31
  203.0 6.1 %fusion.30 = bf16[1,256,8,128]{3,2,1,0:T(8,128)(2,1)S(1)} fusion(bf16[2048,2176]{0,1:T(8,128)(2,1)} %multiply_convert_fusion, bf16[128,128]{1,0:T(8,128)(2,1)S(1)} %copy-done.19, bf16[2048,128]{1,0:T(8,128)(2,1)S(1)} %copy-done.6), kind=kOutput, calls=%fused_computation.32 | convolution fusion | flops 1142489088 | bytes 9994240 | tf_op jit(solution)/shard_map/dot_general | solution.py:31
  209.1 1.1 pad_maximum_fusion.1
  210.2 47.0 %reduce-scatter.7.cloned.1.call-done = bf16[16,256]{1,0:T(8,128)(2,1)} async-done(((bf16[128,256]{1,0:T(8,128)(2,1)}), bf16[16,256]{1,0:T(8,128)(2,1)}) %reduce-scatter.7.cloned.1.call-update) | async-done | bytes 8208
  257.2 0.8 copy.46
  258.0 11.4 %psum.7 = f32[16,256]{0,1:T(8,128)S(1)} all-reduce(bf16[16,256]{0,1:T(8,128)(2,1)S(1)} %copy.46), channel_id=1, replica_groups=mesh['resp'=4,'ctx'=8] {'resp'}, use_global_device_ids=true, to_apply=%region_8.9 | all-reduce | flops 4096 | bytes 24576 | tf_op jit(solution)/shard_map/psum | solution.py:113
  269.5 0.7 copy.37
  270.2 0.7 copy.38
  270.9 56.6 %reduce-scatter.5.cloned.1.call-done = bf16[256,2,256]{2,0,1:T(8,128)(2,1)} async-done(((bf16[2048,2,256]{2,0,1:T(8,128)(2,1)}), bf16[256,2,256]{2,0,1:T(8,128)(2,1)}) %reduce-scatter.5.cloned.1.call-update) | async-done | bytes 262160 | tf_op jit(solution)/shard_map/reduce_scatter | solution.py:103
  327.5 1.7 fusion.60
  (58 shorter events, 0.2 us)
Async XLA Ops:
  7.2 68.6 %all-gather.3.cloned.1.call-start = ((), (), s32[]{:S(2)}) async-start(), calls=%async_computation.2 | async-start | bytes 1179648 | tf_op jit(solution)/shard_map/all_gather | solution.py:56
  7.9 97.6 %all-gather.5.cloned.1.call-start = ((), (), s32[]{:S(2)}) async-start(), calls=%async_computation.3 | async-start | bytes 1179648 | tf_op jit(solution)/shard_map/all_gather | solution.py:57
  8.6 248.6 %reduce-scatter.7.cloned.1.call-start = ((), (), s32[]{:S(2)}) async-start(), calls=%async_computation.5 | async-start | bytes 73728
  41.1 74.2 %copy-start.18 = (bf16[128,128]{1,0:T(8,128)(2,1)}, bf16[128,128]{1,0:T(8,128)(2,1)S(1)}, u32[]{:S(2)}) copy-start(bf16[128,128]{1,0:T(8,128)(2,1)S(1)} %all_gather.12) | copy-start | bytes 98308
  71.9 35.8 %copy-start.13 = (bf16[128,128]{1,0:T(8,128)(2,1)}, bf16[128,128]{1,0:T(8,128)(2,1)S(1)}, u32[]{:S(2)}) copy-start(bf16[128,128]{1,0:T(8,128)(2,1)S(1)} %all_gather.14) | copy-start | bytes 98308
  75.7 76.2 %copy-start = (bf16[2,256,8,128]{3,2,1,0:T(8,128)(2,1)}, bf16[2,256,8,128]{3,2,1,0:T(8,128)(2,1)S(1)}, u32[]{:S(2)}) copy-start(bf16[2,256,8,128]{3,2,1,0:T(8,128)(2,1)S(1)} %multiply_convert_fusion.2) | copy-start | bytes 3145732
  77.4 9.2 %copy-start.7 = (bf16[2048,128]{1,0:T(8,128)(2,1)}, bf16[2048,128]{1,0:T(8,128)(2,1)S(1)}, u32[]{:S(2)}) copy-start(bf16[2048,128]{1,0:T(8,128)(2,1)S(1)} %get-tuple-element.24) | copy-start | bytes 1572868
  77.4 37.9 %copy-start.5 = (bf16[2048,128]{1,0:T(8,128)(2,1)}, bf16[2048,128]{1,0:T(8,128)(2,1)S(1)}, u32[]{:S(2)}) copy-start(bf16[2048,128]{1,0:T(8,128)(2,1)S(1)} %get-tuple-element.25) | copy-start | bytes 1572868
  105.5 9.9 %copy-start.20 = (bf16[2,256,8,128]{3,2,1,0:T(8,128)(2,1)S(1)}, bf16[2,256,8,128]{3,2,1,0:T(8,128)(2,1)}, u32[]{:S(2)}) copy-start(bf16[2,256,8,128]{3,2,1,0:T(8,128)(2,1)} %param.10) | copy-start | bytes 3145732
  105.5 9.9 %copy-start.21 = (s32[2176]{0:T(1024)S(1)}, s32[2176]{0:T(1024)}, u32[]{:S(2)}) copy-start(s32[2176]{0:T(1024)} %constant.8.clone.1) | copy-start | bytes 26116
  107.6 0.8 copy-start.4
  142.2 10.8 %copy-start.3 = (bf16[2048,128]{1,0:T(8,128)(2,1)S(1)}, bf16[2048,128]{1,0:T(8,128)(2,1)}, u32[]{:S(2)}) copy-start(bf16[2048,128]{1,0:T(8,128)(2,1)} %get-tuple-element.22) | copy-start | bytes 1572868
  142.2 10.8 %copy-start.14 = (bf16[128,128]{1,0:T(8,128)(2,1)S(1)}, bf16[128,128]{1,0:T(8,128)(2,1)}, u32[]{:S(2)}) copy-start(bf16[128,128]{1,0:T(8,128)(2,1)} %copy-done.13) | copy-start | bytes 98308
  149.8 5.9 %copy-start.9 = (bf16[2048,128]{1,0:T(8,128)(2,1)S(1)}, bf16[2048,128]{1,0:T(8,128)(2,1)}, u32[]{:S(2)}) copy-start(bf16[2048,128]{1,0:T(8,128)(2,1)} %convolution_convert_fusion.1) | copy-start | bytes 1572868
  149.8 6.8 %slice-start = ((s8[8912896]{0:T(1024)(128)(4,1)}), s8[4194304]{0:T(1024)(128)(4,1)S(1)}, s32[]{:S(2)}) async-start(s8[8912896]{0:T(1024)(128)(4,1)} %bitcast.58), calls=%async_computation.6 | async-start | bytes 8388608
  152.9 2.7 copy-start.1
  153.0 3.7 %slice-start.1 = ((s8[8912896]{0:T(1024)(128)(4,1)}), s8[4194304]{0:T(1024)(128)(4,1)S(1)}, s32[]{:S(2)}) async-start(s8[8912896]{0:T(1024)(128)(4,1)} %bitcast.58), calls=%async_computation.7 | async-start | bytes 8388608
  153.0 3.7 %slice-start.2 = ((s8[8912896]{0:T(1024)(128)(4,1)}), s8[524288]{0:T(1024)(128)(4,1)S(1)}, s32[]{:S(2)}) async-start(s8[8912896]{0:T(1024)(128)(4,1)} %bitcast.58), calls=%async_computation.8 | async-start | bytes 1048576
  179.8 8.5 %copy-start.2 = (bf16[2,256,8,128]{3,2,1,0:T(8,128)(2,1)S(1)}, bf16[2,256,8,128]{3,2,1,0:T(8,128)(2,1)}, u32[]{:S(2)}) copy-start(bf16[2,256,8,128]{3,2,1,0:T(8,128)(2,1)} %copy-done) | copy-start | bytes 3145732
  191.5 2.4 copy-start.15
  191.5 2.4 copy-start.16
  191.5 2.5 copy-start.17
  191.5 3.6 %copy-start.10 = (bf16[2048,128]{1,0:T(8,128)(2,1)S(1)}, bf16[2048,128]{1,0:T(8,128)(2,1)}, u32[]{:S(2)}) copy-start(bf16[2048,128]{1,0:T(8,128)(2,1)} %fusion.25) | copy-start | bytes 1572868
  191.5 3.6 %copy-start.11 = (bf16[2048,128]{1,0:T(8,128)(2,1)S(1)}, bf16[2048,128]{1,0:T(8,128)(2,1)}, u32[]{:S(2)}) copy-start(bf16[2048,128]{1,0:T(8,128)(2,1)} %fusion.22) | copy-start | bytes 1572868
  191.5 3.6 %copy-start.12 = (bf16[2048,128]{1,0:T(8,128)(2,1)S(1)}, bf16[2048,128]{1,0:T(8,128)(2,1)}, u32[]{:S(2)}) copy-start(bf16[2048,128]{1,0:T(8,128)(2,1)} %fusion.16) | copy-start | bytes 1572868
  194.0 2.9 copy-start.8
  194.0 2.9 copy-start.19
  194.8 132.7 %reduce-scatter.5.cloned.1.call-start = ((), (), s32[]{:S(2)}) async-start(), calls=%async_computation.4 | async-start | bytes 2359296 | tf_op jit(solution)/shard_map/reduce_scatter | solution.py:103
  196.8 6.2 %copy-start.6 = (bf16[2048,128]{1,0:T(8,128)(2,1)S(1)}, bf16[2048,128]{1,0:T(8,128)(2,1)}, u32[]{:S(2)}) copy-start(bf16[2048,128]{1,0:T(8,128)(2,1)} %copy-done.5) | copy-start | bytes 1572868
Sparse Core Ops, SparseCore 0:
  10.2 42.8 all-gather.2
  55.3 38.9 all-gather.4
  194.9 62.2 reduce-scatter.6
  260.6 66.8 reduce-scatter.4
where the time goes:
time: 339 us; the launch traced here: 336 us
  waiting for transfers between devices  105 us (31%)
  matrix products  89.7 us (26%)
  blocking collectives  74.4 us (22%)
  other arithmetic  42.5 us (13%)
  between operations  14.5 us (4%)
  local copies, waits for them, and re-layouts  9.5 us (3%)
    reduce_scatter x1, waiting for transfers between devices, per_device(): lax.psum_scatter(jnp.stack(part_list, 1).astype(jnp.bfloat16), 'ctx', sca...  56.6 us
    unnamed x5, waiting for transfers between devices  48.4 us
    all_gather x1, blocking collectives, per_device(): lax.all_gather(prompt_keys, 'ctx', axis=0, tiled=True)  32.4 us
    all_gather x1, blocking collectives, per_device(): lax.all_gather(prompt_values, 'ctx', axis=0, tiled=True)  30.5 us
    dot_general x2, matrix products, attend_block(): jnp.dot(query_rows, keys_all.T, preferred_element_type=jnp.float32)  27.5 us
    convert_element_type x2, other arithmetic, attend_block(): (shifted / jnp.sum(shifted, axis=1, keepdims=True)).astype(jnp.bfloat16)  17.9 us
    dot_general x4, matrix products, member_term(): jnp.dot(score_cols.T, query_rows[member], preferred_element_type=jnp.floa...  17.2 us
    reduce_sum x2, other arithmetic, attend_block(): jnp.sum(shifted, axis=1, keepdims=True)  17 us
  transfers between devices with their start and end apart: 4, of which 2 were waited for; matrix products, arithmetic and copies ran while one was open for 15% of the time, Pallas kernels for 0%

commit v1 on v0

v1 whole, which is shorter than its diff:
```python
import functools
import math

import jax
import jax.numpy as jnp
from jax import lax
from jax.experimental import pallas as pl
from jax.experimental.pallas import tpu as pltpu
from jax.sharding import PartitionSpec as P

RATIO_CAP = 2.0
MASKED = -1e30
SUB_ROWS = 256
TILE_ROWS = 1024
LARGEST_SCORE = 100.0
UNBOUNDED = 3e38

TOP, TOTAL, DOTTED, GUARD, WEIGHT, LENGTH = range(6)
VMEM_BYTES = 24 * 1024 * 1024

NT = (((1,), (1,)), ((), ()))
NN = (((1,), (0,)), ((), ()))


def dot(a, b, dims):
    return lax.dot_general(a, b, dims, preferred_element_type=jnp.float32)


def kinds_of(step, layers):
    if step == 0:
        return ("z",)
    return ("x", "prompt") if step == layers else ("x", "z")


def variants(step, layers, place):
    z, odd = place // 2, place % 2 == 1
    if step == 0:
        return [(None, 0, 1)]
    if step == layers:
        return [(z >= step - 1, 0, 2), (z < step - 1, 1, 2)]
    if step == 1:
        return [
            ((z >= 1) & odd, 0, 2),
            ((z == 0) & odd, 0, 1),
            ((z >= 1) & jnp.logical_not(odd), 1, 2),
        ]
    return [(z >= step, 0, 2), (z == step - 1, 0, 1)]


def attends(step, layers, place):
    if step in (0, layers):
        return place >= 0
    return place >= 1 if step == 1 else place // 2 >= step - 1


def kept_keys(shape, first_row, heads):
    key = lax.broadcasted_iota(jnp.int32, shape, 0)
    row = lax.broadcasted_iota(jnp.int32, shape, 1) + first_row
    return key * heads <= row


def edges_of(counts):
    edges = [0]
    for count in counts:
        edges.append(edges[-1] + count)
    return edges


def largest_norm(rows):
    wide = rows.astype(jnp.float32)
    return jnp.max(jnp.sum(wide * wide, axis=1, keepdims=True))


def filled_tiles(length, tokens, heads, rows):
    per_tile = tile_of(rows) // heads
    left = length - lax.axis_index("ctx") * tokens
    return jnp.clip((left + per_tile - 1) // per_tile, 0, rows // tile_of(rows))


def load_keys(member, pairs, kinds, edges, head_dim, keys, values):
    for part, pair in enumerate(pairs):
        count = edges[part + 1] - edges[part]
        rows = pl.ds(edges[part], count)
        own = pl.ds(0, count)
        if kinds[part] != "prompt":
            own = pl.ds(pl.multiple_of(member * count, count), count)
        keys[rows, :] = pair[own, :head_dim]
        values[rows, :] = pair[own, head_dim:]


def length_of(stat, member):
    return jnp.max(stat[member, LENGTH : LENGTH + 1, 0:128]).astype(jnp.int32)


def spread_weights(ratio, heads):
    tokens = ratio.shape[1]
    shape = (tokens, tokens * heads)
    token = lax.broadcasted_iota(jnp.int32, shape, 0)
    row = lax.broadcasted_iota(jnp.int32, shape, 1)
    first = token * heads
    chosen = jnp.where((row >= first) & (row < first + heads), 1.0, 0.0)
    chosen = chosen.astype(jnp.bfloat16)
    out, rest = None, ratio
    for _ in range(3):
        term = rest.astype(jnp.bfloat16)
        rest = rest - term.astype(jnp.float32)
        few = jnp.broadcast_to(term.astype(jnp.float32), (16, tokens)).astype(jnp.bfloat16)
        part = jnp.dot(few, chosen, preferred_element_type=jnp.float32)[0:1]
        out = part if out is None else out + part
    return out


def forward_kernel(step, layers, heads, head_dim, counts, *refs):
    kinds = kinds_of(step, layers)
    parts = len(kinds)
    earlier = None
    if step == 0:
        lengths, advantages, held_q, held_g, held_behaved, held_current = refs[:6]
        message, out, q, g, keys, values, behaved, current, arrived = refs[6:]
        pairs = [message]
        copies = [
            pltpu.make_async_copy(source, target, arrived.at[i])
            for i, (source, target) in enumerate(
                [(held_behaved, behaved), (held_current, current), (held_q, q), (held_g, g)]
            )
        ]
        for copy in copies:
            copy.start()
        for copy in copies:
            copy.wait()
    else:
        q, g, earlier = refs[:3]
        refs = refs[3:]
        if step == layers:
            messages, (out, prompt, keys, values) = refs[: 2 * layers], refs[2 * layers :]
            own = messages[0].shape[0] - prompt.shape[0] // (2 * layers)
            each = messages[0].shape[0] - own
            for i, message in enumerate(messages):
                prompt[i * each : (i + 1) * each, :] = message[own:, :]
            pairs = [messages[-1], prompt]
        else:
            pairs, (out, keys, values) = refs[:parts], refs[parts:]
    place = lax.axis_index("ctx")
    members, all_rows = q.shape[:2]
    tile = tile_of(all_rows)
    tokens = all_rows // heads
    full_len = tokens * lax.axis_size("ctx")
    scale = head_dim**-0.5 * math.log2(math.e)
    edges = edges_of(counts)
    attended = attends(step, layers, place)

    def shared(member, low, high, first, start):
        rows = pl.ds(pl.multiple_of(first + start, SUB_ROWS), SUB_ROWS)
        scores = dot(keys[low:high, :], q[member, rows, :], NT) * scale
        if step == 0:
            kept = kept_keys(scores.shape, first + start, heads)
            scores = jnp.where(kept, scores, MASKED)
        return rows, scores, dot(values[low:high, :], g[member, rows, :], NT)

    def put(member, rows, top, total, dotted):
        out[member, TOP : TOP + 1, rows] = top
        out[member, TOTAL : TOTAL + 1, rows] = total
        out[member, DOTTED : DOTTED + 1, rows] = dotted

    def bounded(member, low, high, first):
        for start in range(0, tile, SUB_ROWS):
            rows, scores, grad_probs = shared(member, low, high, first, start)
            weight = jnp.exp2(scores)
            total = jnp.sum(weight, axis=0, keepdims=True)
            dotted = jnp.sum(weight * grad_probs, axis=0, keepdims=True)
            if earlier is not None:
                total = total + earlier[member, TOTAL : TOTAL + 1, rows]
                dotted = dotted + earlier[member, DOTTED : DOTTED + 1, rows]
            put(member, rows, jnp.zeros_like(total), total, dotted)

    def general(member, low, high, first):
        for start in range(0, tile, SUB_ROWS):
            rows, scores, grad_probs = shared(member, low, high, first, start)
            top = jnp.max(scores, axis=0, keepdims=True)
            if earlier is not None:
                top = jnp.maximum(top, earlier[member, TOP : TOP + 1, rows])
            weight = jnp.exp2(scores - top)
            total = jnp.sum(weight, axis=0, keepdims=True)
            dotted = jnp.sum(weight * grad_probs, axis=0, keepdims=True)
            if earlier is not None:
                decay = jnp.exp2(earlier[member, TOP : TOP + 1, rows] - top)
                total = total + decay * earlier[member, TOTAL : TOTAL + 1, rows]
                dotted = dotted + decay * earlier[member, DOTTED : DOTTED + 1, rows]
            put(member, rows, top, total, dotted)
            out[member, GUARD : GUARD + 1, rows] = jnp.full_like(total, UNBOUNDED)

    def per_member(member, carry):
        length = lengths[member] if step == 0 else length_of(earlier, member)
        filled = filled_tiles(length, tokens, heads, all_rows)
        if step == 0:
            known = jnp.full((1, all_rows), length).astype(jnp.float32)
            out[member, LENGTH : LENGTH + 1, :] = known

        @pl.when((filled > 0) & attended)
        def _():
            load_keys(member, pairs, kinds, edges, head_dim, keys, values)
            limit = (LARGEST_SCORE / scale) ** 2 / largest_norm(keys[...])

            def per_tile(index, carry):
                first = pl.multiple_of(index * tile, tile)
                rows = pl.ds(first, tile)
                if step == 0:
                    guard = largest_norm(q[member, rows, :])
                    out[member, GUARD : GUARD + 1, rows] = jnp.full((1, tile), guard)
                    count = tile // heads
                    part = pl.ds(pl.multiple_of(index * count, count), count)
                    if count == tokens:
                        part = pl.ds(0, count)
                    ratio = jnp.minimum(jnp.exp(current[:, part] - behaved[:, part]), RATIO_CAP)
                    owner = lax.broadcasted_iota(jnp.int32, ratio.shape, 0)
                    ratio = jnp.sum(
                        jnp.where(owner == member, ratio, 0.0), axis=0, keepdims=True
                    )
                    token = lax.broadcasted_iota(jnp.int32, ratio.shape, 1)
                    position = place * tokens + index * count + token
                    ratio = jnp.where(position < length, ratio, 0.0)
                    spread = full_len / jnp.full((1, 1), length).astype(jnp.float32)
                    ratio = -advantages[member] * ratio * spread
                    out[member, WEIGHT : WEIGHT + 1, rows] = spread_weights(ratio, heads)
                else:
                    guard = jnp.max(earlier[member, GUARD : GUARD + 1, pl.ds(first, 128)])
                fast = guard <= limit
                for condition, begin, past in variants(step, layers, place):
                    low, high = edges[begin], edges[past]
                    for quick, body in ((fast, bounded), (jnp.logical_not(fast), general)):
                        here = quick if condition is None else quick & condition
                        pl.when(here)(functools.partial(body, member, low, high, first))
                return carry

            lax.fori_loop(0, filled, per_tile, 0)

        return carry

    lax.fori_loop(0, members, per_member, 0)


def backward_kernel(step, layers, heads, head_dim, counts, q, g, final, *refs):
    kinds = kinds_of(step, layers)
    count = len(kinds)
    pairs, refs = refs[:count], refs[count:]
    earlier = None
    if step < layers:
        earlier, refs = refs[0], refs[1:]
    grads, query_out, refs = refs[:count], refs[count], refs[count + 1 :]
    keys, values, turned, probs_held, scores_held, sums = refs
    place = lax.axis_index("ctx")
    members, all_rows = q.shape[:2]
    tile = tile_of(all_rows)
    tokens = all_rows // heads
    plain = head_dim**-0.5
    scale = plain * math.log2(math.e)
    edges = edges_of(counts)
    attended = attends(step, layers, place)

    def body(member, low, high, first):
        for start in range(0, tile, SUB_ROWS):
            rows = pl.ds(pl.multiple_of(first + start, SUB_ROWS), SUB_ROWS)
            held = pl.ds(start, SUB_ROWS)
            total = final[member, TOTAL : TOTAL + 1, rows]
            level = final[member, TOP : TOP + 1, rows] + jnp.log2(total)
            delta = final[member, DOTTED : DOTTED + 1, rows] / total
            scores = dot(keys[low:high, :], q[member, rows, :], NT) * scale - level
            if step == 0:
                kept = kept_keys(scores.shape, first + start, heads)
                scores = jnp.where(kept, scores, MASKED)
            probs = jnp.exp2(scores) * final[member, WEIGHT : WEIGHT + 1, rows]
            grad_probs = dot(values[low:high, :], g[member, rows, :], NT)
            grad_scores = (probs * (grad_probs - delta)).astype(jnp.bfloat16)
            probs_held[low:high, held] = probs.astype(jnp.bfloat16)
            scores_held[low:high, held] = grad_scores
            moved = dot(turned[:, low:high], grad_scores, NN)
            if earlier is not None:
                moved = moved + earlier[member, :, rows]
            if step == 0:
                query_out[member, rows, :] = (moved * plain).T.astype(jnp.bfloat16)
            else:
                query_out[member, :, rows] = moved
        rows = pl.ds(first, tile)
        sums[low:high, :head_dim] += dot(scores_held[low:high, :], q[member, rows, :], NN)
        sums[low:high, head_dim:] += dot(probs_held[low:high, :], g[member, rows, :], NN)

    def per_member(member, carry):
        filled = filled_tiles(length_of(final, member), tokens, heads, all_rows)
        filled = jnp.where(attended, filled, 0)
        for part in range(count):
            rows = pl.ds(edges[part], edges[part + 1] - edges[part])

            @pl.when((member == 0) | (kinds[part] != "prompt"))
            def _():
                sums[rows, :] = jnp.zeros_like(sums[rows, :])

        @pl.when(filled > 0)
        def _():
            load_keys(member, pairs, kinds, edges, head_dim, keys, values)
            turned[...] = keys[...].T

            def per_tile(index, carry):
                first = pl.multiple_of(index * tile, tile)
                for condition, begin, past in variants(step, layers, place):
                    run = functools.partial(body, member, edges[begin], edges[past], first)
                    if condition is None:
                        run()
                    else:
                        pl.when(condition)(run)
                return carry

            lax.fori_loop(0, filled, per_tile, 0)

        if step == 0 or earlier is None:

            def clear(index, carry):
                rows = pl.ds(pl.multiple_of(index * tile, tile), tile)
                if step == 0:
                    query_out[member, rows, :] = jnp.zeros((tile, head_dim), jnp.bfloat16)
                else:
                    query_out[member, :, rows] = jnp.zeros((head_dim, tile), jnp.float32)
                return carry

            lax.fori_loop(filled, all_rows // tile, clear, 0)
        for part in range(count):
            if kinds[part] == "prompt":
                continue
            rows = pl.ds(edges[part], counts[part])
            own = pl.ds(pl.multiple_of(member * counts[part], counts[part]), counts[part])
            grads[part][own, :head_dim] = (sums[rows, :head_dim] * plain).astype(jnp.bfloat16)
            grads[part][own, head_dim:] = sums[rows, head_dim:].astype(jnp.bfloat16)
        return carry

    lax.fori_loop(0, members, per_member, 0)
    if step == layers:
        stay, leave = grads[1], grads[0]
        half = stay.shape[0]
        low, middle, high = edges[1], edges[1] + half, edges[2]
        stay[:, :head_dim] = sums[low:middle, :head_dim] * plain
        stay[:, head_dim:] = sums[low:middle, head_dim:]
        far_keys = sums[middle:high, :head_dim] * plain
        own = leave.shape[0] - half
        leave[own:, :head_dim] = far_keys.astype(jnp.bfloat16)
        leave[own:, head_dim:] = sums[middle:high, head_dim:].astype(jnp.bfloat16)


def combine_kernel(step, layers, *refs):
    def wide(ref, rows, columns=slice(None)):
        return ref[rows, columns].astype(jnp.float32)

    if step == layers - 1:
        own, stay, far, out, kept = refs
        count = own.shape[0]
        each = stay.shape[0] // layers
        for j in range(layers):
            before = count + (j - 1) % layers * each
            mine = slice(j * each, (j + 1) * each)
            kept[mine, :] = stay[mine, :] + wide(far, slice(before, before + each))
        out[:count, :] = own[...]
        out[count:, :] = kept[step * each :, :].astype(jnp.bfloat16)
        return
    own, side, above, kept = refs[:4]
    count = own.shape[0]
    each = kept.shape[0] // layers
    mine = slice(step * each, (step + 1) * each)
    prompt = kept[mine, :] + wide(above, slice(count, None))
    rows = slice(0, count)
    total = wide(own, rows) + wide(side, rows) + wide(above, rows)
    if step > 0:
        out = refs[4]
        out[:count, :] = total.astype(jnp.bfloat16)
        out[count:, :] = prompt.astype(jnp.bfloat16)
    else:
        far, key_out, value_out, prompt_out = refs[4:]
        total = (total + wide(far, rows)).astype(jnp.bfloat16)
        head_dim = key_out.shape[1]
        key_out[...] = total[:, :head_dim]
        value_out[...] = total[:, head_dim:]
        prompt_out[...] = prompt


def work(members, rows, columns, head_dim, products):
    return pl.CostEstimate(
        flops=2 * members * rows * columns * head_dim * products,
        bytes_accessed=members * rows * head_dim * 8,
        transcendentals=members * rows * columns,
    )


def tile_of(rows):
    return min(TILE_ROWS, rows)


WHOLE = pl.BlockSpec(memory_space=pltpu.VMEM)
SCALARS = pl.BlockSpec(memory_space=pltpu.SMEM)
PARAMS = pltpu.CompilerParams(vmem_limit_bytes=VMEM_BYTES)


ANYWHERE = pl.BlockSpec(memory_space=pl.ANY)


def forward_step(step, layers, heads, tokens, operands, messages, earlier):
    q = operands[2] if step == 0 else operands[0]
    members, rows, head_dim = q.shape
    each = messages[0].shape[0] - members * tokens
    counts = [tokens] * len(kinds_of(step, layers))
    if step == layers:
        counts[1] = 2 * layers * each
    columns = sum(counts)
    out_shape = [jax.ShapeDtypeStruct((members, 8, rows), jnp.float32)]
    scratch = [pltpu.VMEM((columns, head_dim), jnp.bfloat16)] * 2
    extra = [] if step == 0 else [earlier]
    in_specs = [WHOLE] * 3
    if step == 0:
        in_specs = [SCALARS] * 2 + [ANYWHERE] * 4
        out_shape += [jax.ShapeDtypeStruct(q.shape, q.dtype)] * 2
        small = operands[4]
        scratch += [pltpu.VMEM(small.shape, small.dtype)] * 2
        scratch += [pltpu.SemaphoreType.DMA((4,))]
    elif step == layers:
        out_shape.append(jax.ShapeDtypeStruct((counts[1], 2 * head_dim), jnp.bfloat16))
    return pl.pallas_call(
        functools.partial(forward_kernel, step, layers, heads, head_dim, counts),
        in_specs=in_specs + [WHOLE] * len(messages),
        out_specs=[WHOLE] * len(out_shape),
        out_shape=out_shape,
        scratch_shapes=scratch,
        compiler_params=PARAMS,
        cost_estimate=work(members, rows, columns, head_dim, 2),
        input_output_aliases={} if step == 0 else {2: 0},
        name=f"attend_step{step}",
    )(*operands, *extra, *messages)


def backward_step(step, layers, heads, tokens, each, q, g, final, messages, earlier):
    members, rows, head_dim = q.shape
    counts = [tokens] * len(kinds_of(step, layers))
    block = (members * tokens, 2 * head_dim)
    grad_shapes = [jax.ShapeDtypeStruct(block, jnp.bfloat16)] * len(counts)
    if step == layers:
        counts[1] = 2 * layers * each
        half = layers * each
        grad_shapes = [
            jax.ShapeDtypeStruct((block[0] + half, block[1]), jnp.bfloat16),
            jax.ShapeDtypeStruct((half, block[1]), jnp.float32),
        ]
    columns = sum(counts)
    tile = tile_of(rows)
    if step == 0:
        query_shape = jax.ShapeDtypeStruct(q.shape, jnp.bfloat16)
    else:
        query_shape = jax.ShapeDtypeStruct((members, head_dim, rows), jnp.float32)
    extra = [] if earlier is None else [earlier]
    aliases = {3 + len(messages): len(counts)} if extra and step > 0 else {}
    outs = pl.pallas_call(
        functools.partial(backward_kernel, step, layers, heads, head_dim, counts),
        in_specs=[WHOLE] * (3 + len(messages) + len(extra)),
        out_specs=[WHOLE] * (len(counts) + 1),
        out_shape=grad_shapes + [query_shape],
        scratch_shapes=[pltpu.VMEM((columns, head_dim), jnp.bfloat16)] * 2
        + [pltpu.VMEM((head_dim, columns), jnp.bfloat16)]
        + [pltpu.VMEM((columns, tile), jnp.bfloat16)] * 2
        + [pltpu.VMEM((columns, 2 * head_dim), jnp.float32)],
        compiler_params=PARAMS,
        cost_estimate=work(members, rows, columns, head_dim, 5),
        input_output_aliases=aliases,
        name=f"attend_grad_step{step}",
    )(q, g, final, *messages, *extra)
    return outs[: len(counts)], outs[len(counts)]


def combine(step, layers, each, *terms):
    count, width = terms[0].shape
    if step > 0:
        shapes = [jax.ShapeDtypeStruct((count + each, width), jnp.bfloat16)]
        if step == layers - 1:
            shapes.append(jax.ShapeDtypeStruct((layers * each, width), jnp.float32))
    else:
        shapes = [jax.ShapeDtypeStruct((count, width // 2), jnp.bfloat16)] * 2
        shapes.append(jax.ShapeDtypeStruct((each, width), jnp.float32))
    return pl.pallas_call(
        functools.partial(combine_kernel, step, layers),
        in_specs=[WHOLE] * len(terms),
        out_specs=[WHOLE] * len(shapes),
        out_shape=shapes,
        compiler_params=PARAMS,
        name=f"add_terms{step}",
    )(*terms)


def join_kernel(keys, values, prompt_keys, prompt_values, out, arrived):
    rows, head_dim = keys.shape
    copies = []
    for i, (source, first, column) in enumerate(
        [
            (keys, 0, 0),
            (values, 0, head_dim),
            (prompt_keys, rows, 0),
            (prompt_values, rows, head_dim),
        ]
    ):
        place = out.at[pl.ds(first, source.shape[0]), pl.ds(column, head_dim)]
        copies.append(pltpu.make_async_copy(source, place, arrived.at[i]))
    for copy in copies:
        copy.start()
    for copy in copies:
        copy.wait()


def join(keys, values, prompt_keys, prompt_values):
    rows = keys.shape[0] + prompt_keys.shape[0]
    return pl.pallas_call(
        join_kernel,
        out_shape=jax.ShapeDtypeStruct((rows, 2 * keys.shape[1]), keys.dtype),
        in_specs=[ANYWHERE] * 4,
        out_specs=WHOLE,
        scratch_shapes=[pltpu.SemaphoreType.DMA((4,))],
        compiler_params=PARAMS,
        name="join_pairs",
    )(keys, values, prompt_keys, prompt_values)


def per_device(
    queries,
    prompt_keys,
    prompt_values,
    resp_keys,
    resp_values,
    upstream,
    behav_logp,
    cur_logp,
    advantages,
    lengths,
):
    members, tokens, heads, head_dim = queries.shape
    ctx_size, resp_size = lax.axis_size("ctx"), lax.axis_size("resp")
    layers = ctx_size // 2
    each = prompt_keys.shape[0]
    rows = tokens * heads

    def hop(array, layers_up):
        pairs = [(c, (c + 2 * layers_up) % ctx_size) for c in range(ctx_size)]
        return lax.ppermute(array, "ctx", pairs)

    def cross(array, layers_up=0):
        pairs = [(c, ((c + 2 * layers_up) % ctx_size) ^ 1) for c in range(ctx_size)]
        return lax.ppermute(array, "ctx", pairs)

    z = [
        join(
            resp_keys.reshape(members * tokens, head_dim),
            resp_values.reshape(members * tokens, head_dim),
            prompt_keys,
            prompt_values,
        )
    ]
    x = [None]
    operands = (
        lengths,
        advantages,
        queries.reshape(members, rows, head_dim),
        upstream.reshape(members, rows, head_dim),
        behav_logp,
        cur_logp,
    )
    stat = prompt = None
    for step in range(layers + 1):
        if step < layers:
            held = z[step]
            if step > 0:
                held, stat = lax.optimization_barrier((held, stat))
                z[step] = held
            if step + 1 < layers:
                z.append(hop(held, 1))
                x.append(cross(held))
            if step == 1:
                source, z[1] = lax.optimization_barrier((z[0], z[1]))
                far_message = cross(source, layers - 1)
            if step + 1 == layers:
                x.append(far_message)
        if step == 0:
            stat, q, g = forward_step(0, layers, heads, tokens, operands, z[:1], None)
            operands = (q, g)
        elif step < layers:
            (stat,) = forward_step(
                step, layers, heads, tokens, operands, [x[step], z[step]], stat
            )
        else:
            stat, prompt = forward_step(step, layers, heads, tokens, operands, z + x[1:], stat)

    final = stat
    moved = side = above = far = message = kept = None
    for step in range(layers, -1, -1):
        if message is not None:
            final, message = lax.optimization_barrier((final, message))
            above = hop(message, -1)
        if step == layers:
            messages = [x[step], prompt]
        else:
            messages = [z[0]] if step == 0 else [x[step], z[step]]
        grads, moved = backward_step(
            step, layers, heads, tokens, each, q, g, final, messages, moved
        )
        if step == layers:
            far, stay = cross(grads[0], 1 - layers), grads[1]
            continue
        if step == layers - 1:
            message, kept = combine(step, layers, each, grads[-1], stay, far)
        elif step > 0:
            (message,) = combine(step, layers, each, grads[-1], side, above, kept)
        if step > 0:
            side = cross(grads[0])
    key_grads, value_grads, share = combine(0, layers, each, grads[-1], side, above, kept, far)
    stride = 1
    while stride < resp_size:
        pairs = [(c, c ^ stride) for c in range(resp_size)]
        share = share + lax.ppermute(share, "resp", pairs)
        stride *= 2
    return (
        moved.reshape(queries.shape),
        key_grads.reshape(resp_keys.shape),
        value_grads.reshape(resp_values.shape),
        share[:, :head_dim],
        share[:, head_dim:],
    )


def solution(mesh):
    placed = (
        P("resp", "ctx", None, None),
        P("ctx", None),
        P("ctx", None),
        P("resp", "ctx", None),
        P("resp", "ctx", None),
        P("resp", "ctx", None, None),
        P("resp", "ctx"),
        P("resp", "ctx"),
        P("resp"),
        P("resp"),
    )
    return jax.shard_map(
        per_device,
        mesh=mesh,
        in_specs=placed,
        out_specs=(
            P("resp", "ctx", None, None),
            P("resp", "ctx", None),
            P("resp", "ctx", None),
            P("ctx", None),
            P("ctx", None),
        ),
        check_vma=False,
    )
```

time: 339 us -> 96.1 us (0.28)
  matrix products: 89.7 us -> 0 us
  blocking collectives: 74.4 us -> 0 us
  waiting for transfers between devices: 105 us -> 42.9 us
  other arithmetic: 42.5 us -> 0.01 us
  Pallas kernels: 0 us -> 22.4 us
  starting transfers between devices: 0.41 us -> 21 us
  between operations: 14.5 us -> 0.79 us
    dot_general x16 -> x0, matrix products: 89.7 us -> none  [the longest x2 27.5 us: attend_block(): jnp.dot(query_rows, keys_all.T, preferred_element_type=jnp.float32)]
    all_gather x2 -> x0, blocking collectives: 63 us -> none  [the longest x1 32.4 us: per_device(): lax.all_gather(prompt_keys, 'ctx', axis=0, tiled=True)]
    reduce_scatter x1 -> x0, waiting for transfers between devices: 56.6 us -> none  [per_device(): lax.psum_scatter(jnp.stack(part_list, 1).astype(jnp.bfloat16), 'ctx', sca...]
    unnamed x5 -> x0, waiting for transfers between devices: 48.4 us -> none
    ppermute x0 -> x16, waiting for transfers between devices: none -> 42.9 us  [the longest x8 23.7 us: cross(): return lax.ppermute(array, 'ctx', pairs)]
    pallas_call x0 -> x15, Pallas kernels: none -> 22.4 us  [the longest x5 12.8 us: backward_step(): pl.pallas_call(functools.partial(backward_kernel, step, layers, heads, he...]
    ppermute x0 -> x16, starting transfers between devices: none -> 21 us  [the longest x8 15.3 us: cross(): return lax.ppermute(array, 'ctx', pairs)]
    convert_element_type x4 -> x0, other arithmetic: 19.7 us -> none  [the longest x2 17.9 us: attend_block(): (shifted / jnp.sum(shifted, axis=1, keepdims=True)).astype(jnp.bfloat16)]
  transfers between devices with their start and end apart: 4 -> 16, of which waited for: 2 -> 9; matrix products, arithmetic and copies ran while one was open for 15% -> 0% of each run, Pallas kernels for 0% -> 14%
where the time goes in v1:
time: 96.1 us; the launch traced here: 96 us
  waiting for transfers between devices  42.9 us (45%)
  Pallas kernels  22.4 us (23%)
  starting transfers between devices  21 us (22%)
  local copies, waits for them, and re-layouts  8.9 us (9%)
    ppermute x8, waiting for transfers between devices, cross(): return lax.ppermute(array, 'ctx', pairs)  23.7 us
    ppermute x8, starting transfers between devices, cross(): return lax.ppermute(array, 'ctx', pairs)  15.3 us
    ppermute x6, waiting for transfers between devices, hop(): return lax.ppermute(array, 'ctx', pairs)  15 us
    pallas_call x5, Pallas kernels, backward_step(): pl.pallas_call(functools.partial(backward_kernel, step, layers, heads, he...  12.8 us
    pallas_call x5, Pallas kernels, forward_step(): pl.pallas_call(functools.partial(forward_kernel, step, layers, heads, hea...  8.51 us
    unnamed x20, local copies, waits for them, and re-layouts  8.29 us
    ppermute x6, starting transfers between devices, hop(): return lax.ppermute(array, 'ctx', pairs)  5.02 us
    ppermute x2, waiting for transfers between devices, per_device(): share = share + lax.ppermute(share, 'resp', pairs)  4.22 us
  transfers between devices with their start and end apart: 16, of which 9 were waited for; matrix products, arithmetic and copies ran while one was open for 0% of the time, Pallas kernels for 14%

profile of v1, /device:TPU:0, one launch (start us, length us, event | category | flops | bytes accessed | tf_op | source)
XLA Modules:
  0.0 96.0 jit_solution(7192483693953491555)
XLA Ops:
  0.6 0.9 copy-done.2
  1.5 0.9 copy-done.3
  2.4 0.7 copy-done.4
  3.1 0.7 copy-done.5
  3.8 0.1 join_pairs.1.refs_6_.refs_3_.refs_0_
  3.9 3.1 %collective-permute-start = (bf16[528,256]{1,0:T(8,128)(2,1)S(1)}, bf16[528,256]{1,0:T(8,128)(2,1)S(1)}, u32[]{:S(2)}, u32[]{:S(2)}) collective-permute-start(bf16[528,256]{1,0:T(8,128)(2,1)S(1)} %join_pairs.1.refs_6_.refs_3_.refs_0_), channel_id=1, source_target_pairs={{0,2},{1,3},{2,4},{3,5},{4,6},{5,7},{6,0},{7,1},{8,10},{9,11},{10,... | collective-permute-start | bytes 811016 | tf_op jit(solution)/shard_map/ppermute | solution.py:543
  7.0 1.5 %collective-permute-start.2 = (bf16[528,256]{1,0:T(8,128)(2,1)S(1)}, bf16[528,256]{1,0:T(8,128)(2,1)S(1)}, u32[]{:S(2)}, u32[]{:S(2)}) collective-permute-start(bf16[528,256]{1,0:T(8,128)(2,1)S(1)} %join_pairs.1.refs_6_.refs_3_.refs_0_), channel_id=1, source_target_pairs={{0,1},{1,0},{2,3},{3,2},{4,5},{5,4},{6,7},{7,6},{8,9},{9,8},{10,11... | collective-permute-start | bytes 811016 | tf_op jit(solution)/shard_map/ppermute | solution.py:547
  8.5 1.2 %copy-done = bf16[2,256,8,128]{3,2,1,0:T(8,128)(2,1)S(1)} copy-done((bf16[2,256,8,128]{3,2,1,0:T(8,128)(2,1)S(1)}, bf16[2,256,8,128]{3,2,1,0:T(8,128)(2,1)}, u32[]{:S(2)}) %copy-start) | copy-done | bytes 1048600
  9.7 1.2 %copy-done.1 = bf16[2,256,8,128]{3,2,1,0:T(8,128)(2,1)S(1)} copy-done((bf16[2,256,8,128]{3,2,1,0:T(8,128)(2,1)S(1)}, bf16[2,256,8,128]{3,2,1,0:T(8,128)(2,1)}, u32[]{:S(2)}) %copy-start.1) | copy-done | bytes 1048600
  10.9 0.7 copy-done.6
  11.6 0.7 copy-done.7
  12.3 0.7 copy-done.8
  13.0 0.7 copy-done.9
  13.6 4.9 %attend_step0.1 = (f32[2,8,2048]{2,1,0:T(8,128)S(1)}, bf16[2,2048,128]{2,1,0:T(8,128)(2,1)S(1)}, bf16[2,2048,128]{2,1,0:T(8,128)(2,1)S(1)}) custom-call(s32[2]{0:T(128)S(1)} %copy-done.8, f32[2]{0:T(128)S(1)} %copy-done.9, bf16[2,2048,128]{2,1,0:T(8,128)(2,1)S(1)} %bitcast.7, bf16[2,2048,128]{2,1,0:T(8,128)(2,1)S(1)} %bitcast.8, f32[2,256]{1,0:T(2,128)S(1)} %copy-done.6, ...), custom_call_target="tpu_custom_call" | custom-call | flops 536870912 | bytes 4194304 | tf_op jit(solution)/shard_map/attend_step0/pallas_call | solution.py:422
  18.5 0.0 collective-permute-done.refs_4_.refs_1_
  18.6 1.4 %collective-permute-start.1 = (bf16[528,256]{1,0:T(8,128)(2,1)S(1)}, bf16[528,256]{1,0:T(8,128)(2,1)S(1)}, u32[]{:S(2)}, u32[]{:S(2)}) collective-permute-start(bf16[528,256]{1,0:T(8,128)(2,1)S(1)} %collective-permute-done.refs_4_.refs_1_), channel_id=1, source_target_pairs={{0,2},{1,3},{2,4},{3,5},{4,6},{5,7},{6,0},{7,1},{8,10},{9,11},{10,... | collective-permute-start | bytes 811016 | tf_op jit(solution)/shard_map/ppermute | solution.py:543
  20.0 0.0 collective-permute-start.4
  20.0 0.3 attend_step1.1.refs_2_
  20.2 7.8 %collective-permute-done.1.refs_4_.refs_5_.refs_1_ = bf16[528,256]{1,0:T(8,128)(2,1)S(1)} collective-permute-done((bf16[528,256]{1,0:T(8,128)(2,1)S(1)}, bf16[528,256]{1,0:T(8,128)(2,1)S(1)}, u32[]{:S(2)}, u32[]{:S(2)}) %collective-permute-start.1) | collective-permute-done | bytes 270368 | tf_op jit(solution)/shard_map/ppermute | solution.py:543
  28.1 5.3 %collective-permute-start.6 = (bf16[528,256]{1,0:T(8,128)(2,1)S(1)}, bf16[528,256]{1,0:T(8,128)(2,1)S(1)}, u32[]{:S(2)}, u32[]{:S(2)}) collective-permute-start(bf16[528,256]{1,0:T(8,128)(2,1)S(1)} %join_pairs.1.refs_6_.refs_3_.refs_0_), channel_id=1, source_target_pairs={{0,7},{1,6},{2,1},{3,0},{4,3},{5,2},{6,5},{7,4},{8,15},{9,14},{10,... | collective-permute-start | bytes 811016 | tf_op jit(solution)/shard_map/ppermute | solution.py:547
  33.4 0.3 attend_step2.1.refs_2_
  33.6 5.7 %collective-permute-done.3.refs_4_.refs_6_.refs_1_ = bf16[528,256]{1,0:T(8,128)(2,1)S(1)} collective-permute-done((bf16[528,256]{1,0:T(8,128)(2,1)S(1)}, bf16[528,256]{1,0:T(8,128)(2,1)S(1)}, u32[]{:S(2)}, u32[]{:S(2)}) %collective-permute-start.3) | collective-permute-done | bytes 270368 | tf_op jit(solution)/shard_map/ppermute | solution.py:543
  39.3 1.3 %collective-permute-done.5.refs_3_.refs_9_.refs_0_ = bf16[528,256]{1,0:T(8,128)(2,1)S(1)} collective-permute-done((bf16[528,256]{1,0:T(8,128)(2,1)S(1)}, bf16[528,256]{1,0:T(8,128)(2,1)S(1)}, u32[]{:S(2)}, u32[]{:S(2)}) %collective-permute-start.5) | collective-permute-done | bytes 270368 | tf_op jit(solution)/shard_map/ppermute | solution.py:547
  40.6 0.3 attend_step3.1.refs_2_
  40.9 2.8 %attend_step4.1 = (f32[2,8,2048]{2,1,0:T(8,128)S(1)}, bf16[128,256]{1,0:T(8,128)(2,1)S(1)}) custom-call(bf16[2,2048,128]{2,1,0:T(8,128)(2,1)S(1)} %get-tuple-element.43.refs_0_.q, bf16[2,2048,128]{2,1,0:T(8,128)(2,1)S(1)} %get-tuple-element.44.refs_1_.g, f32[2,8,2048]{2,1,0:T(8,128)S(1)} %attend_step3.1.refs_2_, ...), custom_call_target="tpu_custom_call", output_to_operand_aliasing={{0}: (2, {})} | custom-call | flops 805306368 | bytes 4194304 | tf_op jit(solution)/shard_map/attend_step4/pallas_call | solution.py:422
  43.7 4.8 %attend_grad_step4.1 = (bf16[576,256]{1,0:T(8,128)(2,1)S(1)}, f32[64,256]{1,0:T(8,128)S(1)}, f32[2,128,2048]{2,1,0:T(8,128)S(1)}) custom-call(bf16[2,2048,128]{2,1,0:T(8,128)(2,1)S(1)} %get-tuple-element.43.refs_0_.q, bf16[2,2048,128]{2,1,0:T(8,128)(2,1)S(1)} %get-tuple-element.44.refs_1_.g, f32[2,8,2048]{2,1,0:T(8,128)S(1)} %get-tuple-element.72.final, ...), custom_call_target="tpu_custom_call" | custom-call | flops 2013265920 | bytes 4194304 | tf_op jit(solution)/shard_map/attend_grad_step4/pallas_call | solution.py:455
  48.5 0.3 collective-permute-start.7
  48.8 0.4 attend_grad_step3.1
  49.2 11.6 %collective-permute-done.7.refs_2_.refs_4_ = bf16[576,256]{1,0:T(8,128)(2,1)S(1)} collective-permute-done((bf16[576,256]{1,0:T(8,128)(2,1)S(1)}, bf16[576,256]{1,0:T(8,128)(2,1)S(1)}, u32[]{:S(2)}, u32[]{:S(2)}) %collective-permute-start.7) | collective-permute-done | bytes 294944 | tf_op jit(solution)/shard_map/ppermute | solution.py:547
  60.8 0.1 collective-permute-start.9
  60.9 1.4 %collective-permute-start.8 = (bf16[512,256]{1,0:T(8,128)(2,1)S(1)}, bf16[512,256]{1,0:T(8,128)(2,1)S(1)}, u32[]{:S(2)}, u32[]{:S(2)}) collective-permute-start(bf16[512,256]{1,0:T(8,128)(2,1)S(1)} %get-tuple-element.64), channel_id=1, source_target_pairs={{0,1},{1,0},{2,3},{3,2},{4,5},{5,4},{6,7},{7,6},{8,9},{9,8},{10,11... | collective-permute-start | bytes 786440 | tf_op jit(solution)/shard_map/ppermute | solution.py:547
  62.3 0.3 attend_grad_step2.1
  62.6 4.7 %collective-permute-done.8.refs_1_ = bf16[512,256]{1,0:T(8,128)(2,1)S(1)} collective-permute-done((bf16[512,256]{1,0:T(8,128)(2,1)S(1)}, bf16[512,256]{1,0:T(8,128)(2,1)S(1)}, u32[]{:S(2)}, u32[]{:S(2)}) %collective-permute-start.8) | collective-permute-done | bytes 262176 | tf_op jit(solution)/shard_map/ppermute | solution.py:547
  67.3 1.5 %collective-permute-done.9.refs_2_ = bf16[528,256]{1,0:T(8,128)(2,1)S(1)} collective-permute-done((bf16[528,256]{1,0:T(8,128)(2,1)S(1)}, bf16[528,256]{1,0:T(8,128)(2,1)S(1)}, u32[]{:S(2)}, u32[]{:S(2)}) %collective-permute-start.9) | collective-permute-done | bytes 270368 | tf_op jit(solution)/shard_map/ppermute | solution.py:543
  68.8 0.1 add_terms2.1
  68.9 0.4 collective-permute-start.11
  69.3 2.6 %collective-permute-start.10 = (bf16[512,256]{1,0:T(8,128)(2,1)S(1)}, bf16[512,256]{1,0:T(8,128)(2,1)S(1)}, u32[]{:S(2)}, u32[]{:S(2)}) collective-permute-start(bf16[512,256]{1,0:T(8,128)(2,1)S(1)} %get-tuple-element.70), channel_id=1, source_target_pairs={{0,1},{1,0},{2,3},{3,2},{4,5},{5,4},{6,7},{7,6},{8,9},{9,8},{10,11... | collective-permute-start | bytes 786440 | tf_op jit(solution)/shard_map/ppermute | solution.py:547
  71.9 0.3 attend_grad_step1.1
  72.2 6.1 %collective-permute-done.10.refs_1_ = bf16[512,256]{1,0:T(8,128)(2,1)S(1)} collective-permute-done((bf16[512,256]{1,0:T(8,128)(2,1)S(1)}, bf16[512,256]{1,0:T(8,128)(2,1)S(1)}, u32[]{:S(2)}, u32[]{:S(2)}) %collective-permute-start.10) | collective-permute-done | bytes 262176 | tf_op jit(solution)/shard_map/ppermute | solution.py:547
  78.3 0.1 add_terms1.1
  78.4 0.1 collective-permute-start.13
  78.5 4.2 %collective-permute-start.12 = (bf16[512,256]{1,0:T(8,128)(2,1)S(1)}, bf16[512,256]{1,0:T(8,128)(2,1)S(1)}, u32[]{:S(2)}, u32[]{:S(2)}) collective-permute-start(bf16[512,256]{1,0:T(8,128)(2,1)S(1)} %get-tuple-element.76), channel_id=1, source_target_pairs={{0,1},{1,0},{2,3},{3,2},{4,5},{5,4},{6,7},{7,6},{8,9},{9,8},{10,11... | collective-permute-start | bytes 786440 | tf_op jit(solution)/shard_map/ppermute | solution.py:547
  82.7 6.9 %attend_grad_step0.1 = (bf16[512,256]{1,0:T(8,128)(2,1)S(1)}, bf16[2,2048,128]{2,1,0:T(8,128)(2,1)}) custom-call(bf16[2,2048,128]{2,1,0:T(8,128)(2,1)S(1)} %get-tuple-element.43.refs_0_.q, bf16[2,2048,128]{2,1,0:T(8,128)(2,1)S(1)} %get-tuple-element.44.refs_1_.g, f32[2,8,2048]{2,1,0:T(8,128)S(1)} %get-tuple-element.72.final, ...), custom_call_target="tpu_custom_call" | custom-call | flops 1342177280 | bytes 4194304 | tf_op jit(solution)/shard_map/attend_grad_step0/pallas_call | solution.py:455
  89.7 0.8 add_terms0.1
  90.5 1.2 %collective-permute-done.14 = f32[16,256]{1,0:T(8,128)S(1)} collective-permute-done((f32[16,256]{1,0:T(8,128)S(1)}, f32[16,256]{1,0:T(8,128)S(1)}, u32[]{:S(2)}, u32[]{:S(2)}) %collective-permute-start.14) | collective-permute-done | bytes 16416 | tf_op jit(solution)/shard_map/ppermute | solution.py:617
  91.7 0.7 collective-permute-start.15
  92.4 3.0 %collective-permute-done.15 = f32[16,256]{1,0:T(8,128)S(1)} collective-permute-done((f32[16,256]{1,0:T(8,128)S(1)}, f32[16,256]{1,0:T(8,128)S(1)}, u32[]{:S(2)}, u32[]{:S(2)}) %collective-permute-start.15) | collective-permute-done | bytes 16416 | tf_op jit(solution)/shard_map/ppermute | solution.py:617
  95.4 0.6 fusion
  (22 shorter events, 0.1 us)
Async XLA Ops:
  0.6 0.9 copy-start.2
  1.5 0.9 copy-start.3
  2.4 0.7 copy-start.4
  3.1 0.7 copy-start.5
  3.9 14.6 %collective-permute-start = (bf16[528,256]{1,0:T(8,128)(2,1)S(1)}, bf16[528,256]{1,0:T(8,128)(2,1)S(1)}, u32[]{:S(2)}, u32[]{:S(2)}) collective-permute-start(bf16[528,256]{1,0:T(8,128)(2,1)S(1)} %join_pairs.1.refs_6_.refs_3_.refs_0_), channel_id=1, source_target_pairs={{0,2},{1,3},{2,4},{3,5},{4,6},{5,7},{6,0},{7,1},{8,10},{9,11},{10,... | collective-permute-start | bytes 811016 | tf_op jit(solution)/shard_map/ppermute | solution.py:543
  7.0 13.0 %collective-permute-start.2 = (bf16[528,256]{1,0:T(8,128)(2,1)S(1)}, bf16[528,256]{1,0:T(8,128)(2,1)S(1)}, u32[]{:S(2)}, u32[]{:S(2)}) collective-permute-start(bf16[528,256]{1,0:T(8,128)(2,1)S(1)} %join_pairs.1.refs_6_.refs_3_.refs_0_), channel_id=1, source_target_pairs={{0,1},{1,0},{2,3},{3,2},{4,5},{5,4},{6,7},{7,6},{8,9},{9,8},{10,11... | collective-permute-start | bytes 811016 | tf_op jit(solution)/shard_map/ppermute | solution.py:547
  8.5 1.2 %copy-start = (bf16[2,256,8,128]{3,2,1,0:T(8,128)(2,1)S(1)}, bf16[2,256,8,128]{3,2,1,0:T(8,128)(2,1)}, u32[]{:S(2)}) copy-start(bf16[2,256,8,128]{3,2,1,0:T(8,128)(2,1)} %param.10) | copy-start | bytes 3145732
  9.7 1.2 %copy-start.1 = (bf16[2,256,8,128]{3,2,1,0:T(8,128)(2,1)S(1)}, bf16[2,256,8,128]{3,2,1,0:T(8,128)(2,1)}, u32[]{:S(2)}) copy-start(bf16[2,256,8,128]{3,2,1,0:T(8,128)(2,1)} %param.15) | copy-start | bytes 3145732
  10.9 0.7 copy-start.6
  11.6 0.7 copy-start.7
  12.3 0.7 copy-start.8
  13.0 0.7 copy-start.9
  18.6 9.5 %collective-permute-start.1 = (bf16[528,256]{1,0:T(8,128)(2,1)S(1)}, bf16[528,256]{1,0:T(8,128)(2,1)S(1)}, u32[]{:S(2)}, u32[]{:S(2)}) collective-permute-start(bf16[528,256]{1,0:T(8,128)(2,1)S(1)} %collective-permute-done.refs_4_.refs_1_), channel_id=1, source_target_pairs={{0,2},{1,3},{2,4},{3,5},{4,6},{5,7},{6,0},{7,1},{8,10},{9,11},{10,... | collective-permute-start | bytes 811016 | tf_op jit(solution)/shard_map/ppermute | solution.py:543
  20.0 13.4 %collective-permute-start.4 = (bf16[528,256]{1,0:T(8,128)(2,1)S(1)}, bf16[528,256]{1,0:T(8,128)(2,1)S(1)}, u32[]{:S(2)}, u32[]{:S(2)}) collective-permute-start(bf16[528,256]{1,0:T(8,128)(2,1)S(1)} %collective-permute-done.refs_4_.refs_1_), channel_id=1, source_target_pairs={{0,1},{1,0},{2,3},{3,2},{4,5},{5,4},{6,7},{7,6},{8,9},{9,8},{10,11... | collective-permute-start | bytes 811016 | tf_op jit(solution)/shard_map/ppermute | solution.py:547
  28.1 11.2 %collective-permute-start.3 = (bf16[528,256]{1,0:T(8,128)(2,1)S(1)}, bf16[528,256]{1,0:T(8,128)(2,1)S(1)}, u32[]{:S(2)}, u32[]{:S(2)}) collective-permute-start(bf16[528,256]{1,0:T(8,128)(2,1)S(1)} %collective-permute-done.1.refs_4_.refs_5_.refs_1_), channel_id=1, source_target_pairs={{0,2},{1,3},{2,4},{3,5},{4,6},{5,7},{6,0},{7,1},{8,10},{9,11},{10,... | collective-permute-start | bytes 811016 | tf_op jit(solution)/shard_map/ppermute | solution.py:543
  28.1 12.5 %collective-permute-start.5 = (bf16[528,256]{1,0:T(8,128)(2,1)S(1)}, bf16[528,256]{1,0:T(8,128)(2,1)S(1)}, u32[]{:S(2)}, u32[]{:S(2)}) collective-permute-start(bf16[528,256]{1,0:T(8,128)(2,1)S(1)} %collective-permute-done.1.refs_4_.refs_5_.refs_1_), channel_id=1, source_target_pairs={{0,1},{1,0},{2,3},{3,2},{4,5},{5,4},{6,7},{7,6},{8,9},{9,8},{10,11... | collective-permute-start | bytes 811016 | tf_op jit(solution)/shard_map/ppermute | solution.py:547
  28.1 12.8 %collective-permute-start.6 = (bf16[528,256]{1,0:T(8,128)(2,1)S(1)}, bf16[528,256]{1,0:T(8,128)(2,1)S(1)}, u32[]{:S(2)}, u32[]{:S(2)}) collective-permute-start(bf16[528,256]{1,0:T(8,128)(2,1)S(1)} %join_pairs.1.refs_6_.refs_3_.refs_0_), channel_id=1, source_target_pairs={{0,7},{1,6},{2,1},{3,0},{4,3},{5,2},{6,5},{7,4},{8,15},{9,14},{10,... | collective-permute-start | bytes 811016 | tf_op jit(solution)/shard_map/ppermute | solution.py:547
  48.5 12.3 %collective-permute-start.7 = (bf16[576,256]{1,0:T(8,128)(2,1)S(1)}, bf16[576,256]{1,0:T(8,128)(2,1)S(1)}, u32[]{:S(2)}, u32[]{:S(2)}) collective-permute-start(bf16[576,256]{1,0:T(8,128)(2,1)S(1)} %get-tuple-element.59), channel_id=1, source_target_pairs={{0,3},{1,2},{2,5},{3,4},{4,7},{5,6},{6,1},{7,0},{8,11},{9,10},{10,... | collective-permute-start | bytes 884744 | tf_op jit(solution)/shard_map/ppermute | solution.py:547
  60.8 8.0 %collective-permute-start.9 = (bf16[528,256]{1,0:T(8,128)(2,1)S(1)}, bf16[528,256]{1,0:T(8,128)(2,1)S(1)}, u32[]{:S(2)}, u32[]{:S(2)}) collective-permute-start(bf16[528,256]{1,0:T(8,128)(2,1)S(1)} %get-tuple-element.65), channel_id=1, source_target_pairs={{0,6},{1,7},{2,0},{3,1},{4,2},{5,3},{6,4},{7,5},{8,14},{9,15},{10,... | collective-permute-start | bytes 811016 | tf_op jit(solution)/shard_map/ppermute | solution.py:543
  60.9 6.4 %collective-permute-start.8 = (bf16[512,256]{1,0:T(8,128)(2,1)S(1)}, bf16[512,256]{1,0:T(8,128)(2,1)S(1)}, u32[]{:S(2)}, u32[]{:S(2)}) collective-permute-start(bf16[512,256]{1,0:T(8,128)(2,1)S(1)} %get-tuple-element.64), channel_id=1, source_target_pairs={{0,1},{1,0},{2,3},{3,2},{4,5},{5,4},{6,7},{7,6},{8,9},{9,8},{10,11... | collective-permute-start | bytes 786440 | tf_op jit(solution)/shard_map/ppermute | solution.py:547
  68.9 9.5 %collective-permute-start.11 = (bf16[528,256]{1,0:T(8,128)(2,1)S(1)}, bf16[528,256]{1,0:T(8,128)(2,1)S(1)}, u32[]{:S(2)}, u32[]{:S(2)}) collective-permute-start(bf16[528,256]{1,0:T(8,128)(2,1)S(1)} %add_terms2.1), channel_id=1, source_target_pairs={{0,6},{1,7},{2,0},{3,1},{4,2},{5,3},{6,4},{7,5},{8,14},{9,15},{10,... | collective-permute-start | bytes 811016 | tf_op jit(solution)/shard_map/ppermute | solution.py:543
  69.3 9.1 %collective-permute-start.10 = (bf16[512,256]{1,0:T(8,128)(2,1)S(1)}, bf16[512,256]{1,0:T(8,128)(2,1)S(1)}, u32[]{:S(2)}, u32[]{:S(2)}) collective-permute-start(bf16[512,256]{1,0:T(8,128)(2,1)S(1)} %get-tuple-element.70), channel_id=1, source_target_pairs={{0,1},{1,0},{2,3},{3,2},{4,5},{5,4},{6,7},{7,6},{8,9},{9,8},{10,11... | collective-permute-start | bytes 786440 | tf_op jit(solution)/shard_map/ppermute | solution.py:547
  78.4 11.2 %collective-permute-start.13 = (bf16[528,256]{1,0:T(8,128)(2,1)S(1)}, bf16[528,256]{1,0:T(8,128)(2,1)S(1)}, u32[]{:S(2)}, u32[]{:S(2)}) collective-permute-start(bf16[528,256]{1,0:T(8,128)(2,1)S(1)} %add_terms1.1), channel_id=1, source_target_pairs={{0,6},{1,7},{2,0},{3,1},{4,2},{5,3},{6,4},{7,5},{8,14},{9,15},{10,... | collective-permute-start | bytes 811016 | tf_op jit(solution)/shard_map/ppermute | solution.py:543
  78.5 11.1 %collective-permute-start.12 = (bf16[512,256]{1,0:T(8,128)(2,1)S(1)}, bf16[512,256]{1,0:T(8,128)(2,1)S(1)}, u32[]{:S(2)}, u32[]{:S(2)}) collective-permute-start(bf16[512,256]{1,0:T(8,128)(2,1)S(1)} %get-tuple-element.76), channel_id=1, source_target_pairs={{0,1},{1,0},{2,3},{3,2},{4,5},{5,4},{6,7},{7,6},{8,9},{9,8},{10,11... | collective-permute-start | bytes 786440 | tf_op jit(solution)/shard_map/ppermute | solution.py:547
  90.5 1.2 %collective-permute-start.14 = (f32[16,256]{1,0:T(8,128)S(1)}, f32[16,256]{1,0:T(8,128)S(1)}, u32[]{:S(2)}, u32[]{:S(2)}) collective-permute-start(f32[16,256]{1,0:T(8,128)S(1)} %get-tuple-element.80), channel_id=1, source_target_pairs={{0,8},{8,0},{16,24},{24,16},{1,9},{9,1},{17,25},{25,17},{2,10},{10... | collective-permute-start | bytes 49160 | tf_op jit(solution)/shard_map/ppermute | solution.py:617
  91.7 3.7 %collective-permute-start.15 = (f32[16,256]{1,0:T(8,128)S(1)}, f32[16,256]{1,0:T(8,128)S(1)}, u32[]{:S(2)}, u32[]{:S(2)}) collective-permute-start(f32[16,256]{1,0:T(8,128)S(1)} %add.6), channel_id=1, source_target_pairs={{0,16},{8,24},{16,0},{24,8},{1,17},{9,25},{17,1},{25,9},{2,18},{10... | collective-permute-start | bytes 49160 | tf_op jit(solution)/shard_map/ppermute | solution.py:617
